TPU v7x, 32 devices: a whole 2x2x4 slice. The times are simulated.
32 devices in a mesh: pole: 4 (over y, x), row: 2 (over core), col: 4 (over z).
Axes of the slice: x: 2, y: 2, z: 4, core: 2. Of those that a mesh axis runs over, the one named last changes fastest.
Arguments:
- hamiltonian_panel: bfloat16 [6144, 512], P(('row', 'col'), 'pole'), may hold values from -0.005859375 to 0.005859375
- margin_panel: bfloat16 [6144, 512], P(('row', 'col'), 'pole'), may hold values from -0.0029296875 to 0.0029296875
- shifts: float32 [4, 2], P('pole'), may hold values from -2 to 2
- weights: float32 [4, 2], P('pole'), may hold values from 0.5 to 2
- pivot_inverse: float32 [4, 2, 512, 512], P('pole'), may hold values from -6 to 6
- selected_inverse: bfloat16 [4, 2, 6144, 6144], P('pole', None, 'row', 'col'), may hold values from -6 to 6
Outputs:
- inverse_column: float32 [4, 6144, 2, 512], P('pole', ('row', 'col'))
- inverse_pivot: float32 [4, 2, 512, 512], P('pole')
- density_column: float32 [6144, 512], P(('row', 'col'), 'pole')
- density_pivot: float32 [512, 512], P('pole')
All inputs are finite; a program needn't handle non-finite values.
Results may differ from a plain program's by a relative error of at most 0.0037.
Values may be sent and summed in bfloat16 or wider, within the bound.
A program may use at most 128 MiB of HBM per device.

v0:
```python
import jax
import jax.numpy as jnp
from jax import lax
from jax.sharding import PartitionSpec as P

PANEL = 512


def precise(left, right):
    return jnp.dot(left, right, precision=lax.Precision.HIGHEST, preferred_element_type=jnp.float32)


def factor_panel(hamiltonian, margin, shift, inverse):
    hamiltonian_f = hamiltonian.astype(jnp.float32)
    margin_f = margin.astype(jnp.float32)
    real_part = hamiltonian_f - shift[0] * margin_f
    imag_part = -shift[1] * margin_f
    lower_real = precise(real_part, inverse[0]) - precise(imag_part, inverse[1])
    lower_imag = precise(real_part, inverse[1]) + precise(imag_part, inverse[0])
    return jnp.stack([lower_real, lower_imag], axis=1).astype(jnp.bfloat16)


def apply_block(block_real, block_imag, lower):
    width = lower.shape[2]
    flat = lower.reshape(lower.shape[0], 2 * width)
    first = jnp.dot(block_real, flat, preferred_element_type=jnp.float32)
    second = jnp.dot(block_imag, flat, preferred_element_type=jnp.float32)
    return -jnp.stack(
        [first[:, :width] - second[:, width:], first[:, width:] + second[:, :width]], axis=1
    )


def pivot_term(lower, column):
    width = lower.shape[2]
    left = lower.astype(jnp.float32).reshape(lower.shape[0], 2 * width)
    right = column.reshape(column.shape[0], 2 * width)
    square = lax.dot_general(
        left,
        right,
        (((0,), (0,)), ((), ())),
        precision=lax.Precision.HIGHEST,
        preferred_element_type=jnp.float32,
    )
    return jnp.stack(
        [
            square[:width, :width] - square[width:, width:],
            square[:width, width:] + square[width:, :width],
        ]
    )


def body(hamiltonian_panel, margin_panel, shifts, weights, pivot_inverse, selected_inverse):
    shift = shifts[0]
    weight = weights[0]
    inverse = pivot_inverse[0]
    block = selected_inverse[0]
    span = block.shape[2]
    column_index = lax.axis_index("col")
    both = (
        lax.all_gather(hamiltonian_panel, "pole", axis=1, tiled=True),
        lax.all_gather(margin_panel, "pole", axis=1, tiled=True),
    )
    owned = factor_panel(both[0], both[1], shift, inverse)
    gathered = lax.all_gather(owned, ("row", "col"), axis=0, tiled=True)
    needed = lax.dynamic_slice_in_dim(gathered, column_index * span, span, 0)
    block_real = block[0]
    block_imag = block[1]
    column = lax.psum_scatter(
        apply_block(block_real, block_imag, needed), "col", scatter_dimension=0, tiled=True
    )
    pivot = inverse - lax.psum(pivot_term(owned, column), ("row", "col"))
    column_density = weight[0] * column[:, 0] - weight[1] * column[:, 1]
    pivot_density = weight[0] * pivot[0] - weight[1] * pivot[1]
    totals = lax.psum((column_density, pivot_density), "pole")
    portion = PANEL // lax.axis_size("pole")
    slot = lax.axis_index("pole")
    column_share = lax.dynamic_slice_in_dim(totals[0], slot * portion, portion, 1)
    pivot_share = lax.dynamic_slice_in_dim(totals[1], slot * portion, portion, 0)
    return (column[None], pivot[None], column_share, pivot_share)


def solution(mesh):
    return jax.shard_map(
        body,
        mesh=mesh,
        in_specs=(
            P(("row", "col"), "pole"),
            P(("row", "col"), "pole"),
            P("pole", None),
            P("pole", None),
            P("pole", None, None, None),
            P("pole", None, "row", "col"),
        ),
        out_specs=(
            P("pole", ("row", "col"), None, None),
            P("pole", None, None, None),
            P(("row", "col"), "pole"),
            P("pole", None),
        ),
        check_vma=False,
    )
```

profile of v0, /device:TPU:0, one launch (start us, length us, event | category | flops | bytes accessed | tf_op | source)
XLA Modules:
  0.0 594.3 jit_solution(16487910491604722457)
XLA Ops:
  7.2 13.8 %all_gather.10 = bf16[768,512]{1,0:T(8,128)(2,1)S(1)} all-gather(bf16[768,128]{1,0:T(8,128)(2,1)} %param.7), channel_id=1, replica_groups=mesh['pole'=4,'row'=2,'col'=4] {'pole'}, dimensions={1}, use_global_device_ids=true | all-gather | bytes 983040 | tf_op jit(solution)/shard_map/all_gather | solution.py:61
  21.0 1.3 fusion.42
  22.3 11.1 %all_gather.9 = bf16[768,512]{1,0:T(8,128)(2,1)S(1)} all-gather(bf16[768,128]{1,0:T(8,128)(2,1)} %param.6), channel_id=1, replica_groups=mesh['pole'=4,'row'=2,'col'=4] {'pole'}, dimensions={1}, use_global_device_ids=true | all-gather | bytes 983040 | tf_op jit(solution)/shard_map/all_gather | solution.py:60
  33.4 5.0 fusion.21
  38.4 3.7 fusion.19
  42.8 3.1 fusion.23
  45.8 3.1 fusion.24
  48.9 1.5 pad_maximum_fusion.1
  50.4 117.1 %all-gather.2.cloned.1.call-done = bf16[6144,2,512]{0,2,1:T(8,128)(2,1)} async-done(((bf16[768,2,512]{0,2,1:T(8,128)(2,1)}), bf16[6144,2,512]{0,2,1:T(8,128)(2,1)}) %all-gather.2.cloned.1.call-update) | async-done | bytes 12582928 | tf_op jit(solution)/shard_map/all_gather | solution.py:64
  167.5 2.1 constant_dynamic-slice_fusion.2
  169.6 12.5 %fusion.6 = f32[3072,1024]{0,1:T(8,128)S(1)} fusion(bf16[1536,1024]{0,1:T(8,128)(2,1)S(1)} %bitcast.59, bf16[1,2,3072,1536]{3,2,1,0:T(8,128)(2,1)} %param.11), kind=kOutput, calls=%fused_computation.7 | convolution fusion | flops 9663676416 | bytes 25165824 | tf_op jit(solution)/shard_map/dot_general | solution.py:26
  182.1 15.2 %fusion.9 = f32[3072,1024]{0,1:T(8,128)} fusion(bf16[1536,1024]{0,1:T(8,128)(2,1)S(1)} %bitcast.60, bf16[1,2,3072,1536]{3,2,1,0:T(8,128)(2,1)} %param.11), kind=kOutput, calls=%fused_computation.8 | convolution fusion | flops 9663676416 | bytes 25165824 | tf_op jit(solution)/shard_map/dot_general | solution.py:27
  197.3 7.4 %fusion.13 = (f32[3072,1,512]{0,2,1:T(8,128)S(1)}, f32[3072,1,512]{0,2,1:T(8,128)}) fusion(f32[3072,1024]{0,1:T(8,128)} %fusion.9, f32[3072,1024]{0,1:T(8,128)S(1)} %fusion.6), kind=kLoop, calls=%fused_computation.12 | loop fusion | flops 3145728 | bytes 37748736 | tf_op jit(solution)/shard_map/stack | solution.py:28
  204.8 9.2 %maximum_negate_fusion = f32[3072,2,512]{0,2,1:T(8,128)} fusion(f32[3072,1,512]{0,2,1:T(8,128)} %get-tuple-element.11, f32[3072,1,512]{0,2,1:T(8,128)S(1)} %get-tuple-element.10), kind=kLoop, calls=%fused_computation | loop fusion | flops 6291456 | bytes 25165824 | tf_op jit(solution)/shard_map/neg | solution.py:28
  214.0 0.3 all-reduce.4.cloned.1.call-start
  214.2 209.9 %reduce-scatter.2.cloned.1.call-done = f32[768,2,512]{0,2,1:T(8,128)} async-done(((f32[3072,2,512]{0,2,1:T(8,128)}), f32[768,2,512]{0,2,1:T(8,128)}) %reduce-scatter.2.cloned.1.call-update) | async-done | bytes 3145744 | tf_op jit(solution)/shard_map/reduce_scatter | solution.py:68
  424.2 7.1 %fusion.43 = f32[1024,1024]{1,0:T(8,128)S(1)} fusion(bf16[768,1024]{0,1:T(8,128)(2,1)S(1)} %bitcast.58, f32[768,1024]{0,1:T(8,128)} %bitcast.55), kind=kOutput, calls=%fused_computation.56 | convolution fusion | flops 9663676416 | bytes 8912896 | tf_op jit(solution)/shard_map/dot_general | solution.py:37
  431.3 0.5 fusion.28
  431.8 1.5 pad_maximum_fusion
  433.4 0.0 all-reduce.6.cloned.1.call-start
  433.4 0.6 copy-done.5
  434.0 0.6 fusion.41
  434.6 4.7 fusion.18
  439.3 60.3 %all-reduce.4.cloned.1.call-done = f32[2,512,512]{2,1,0:T(8,128)} async-done(((f32[2,512,512]{2,1,0:T(8,128)}), f32[2,512,512]{2,1,0:T(8,128)}) %all-reduce.4.cloned.1.call-update) | async-done | bytes 2097168 | tf_op jit(solution)/shard_map/psum | solution.py:71
  499.5 2.1 bitcast_subtract_fusion
  501.6 1.3 copy-done.3
  502.9 2.8 fusion.26
  505.8 3.4 copy.10
  509.1 75.0 %all-reduce.6.cloned.1.call-done = (f32[768,512]{0,1:T(8,128)}, f32[512,512]{1,0:T(8,128)}) async-done(((f32[768,512]{0,1:T(8,128)}, f32[512,512]{1,0:T(8,128)}), (f32[768,512]{0,1:T(8,128)}, f32[512,512]{1,0:T(8,128)})) %all-reduce.6.cloned.1.call-update) | async-done | bytes 2621456 | tf_op jit(solution)/shard_map/psum | solution.py:74
  584.2 1.0 constant_dynamic-slice_fusion.1
  585.2 0.9 copy.11
  586.1 1.7 constant_dynamic-slice_fusion
  (16 shorter events, 0.2 us)
Async XLA Ops:
  7.2 160.4 %all-gather.2.cloned.1.call-start = ((), (), s32[]{:S(2)}) async-start(), calls=%async_computation.1 | async-start | bytes 14155776 | tf_op jit(solution)/shard_map/all_gather | solution.py:64
  33.4 5.0 copy-start
  50.4 373.8 %reduce-scatter.2.cloned.1.call-start = ((), (), s32[]{:S(2)}) async-start(), calls=%async_computation.2 | async-start | bytes 15728640 | tf_op jit(solution)/shard_map/reduce_scatter | solution.py:68
  213.9 210.2 %copy-start.4 = (bf16[768,2,512]{0,2,1:T(8,128)(2,1)S(1)}, bf16[768,2,512]{0,2,1:T(8,128)(2,1)}, u32[]{:S(2)}) copy-start(bf16[768,2,512]{0,2,1:T(8,128)(2,1)} %pad_maximum_fusion.1) | copy-start | bytes 4718596
  214.0 285.5 %all-reduce.4.cloned.1.call-start = ((), (), s32[]{:S(2)}) async-start(), calls=%async_computation.3 | async-start | bytes 4194304 | tf_op jit(solution)/shard_map/psum | solution.py:71
  433.3 0.7 copy-start.5
  433.4 150.8 %all-reduce.6.cloned.1.call-start = ((), (), s32[]{:S(2)}) async-start(), calls=%async_computation.4 | async-start | bytes 5242880 | tf_op jit(solution)/shard_map/psum | solution.py:74
  434.6 64.9 %copy-start.1 = (f32[1,2,512,512]{3,2,1,0:T(8,128)S(1)}, f32[1,2,512,512]{3,2,1,0:T(8,128)}, u32[]{:S(2)}) copy-start(f32[1,2,512,512]{3,2,1,0:T(8,128)} %param.10) | copy-start | bytes 6291460
  501.6 1.3 copy-start.3
  502.9 2.9 copy-start.2
Sparse Core Ops, SparseCore 0:
  50.5 116.9 all-gather.1
  214.1 210.0 reduce-scatter.1
  433.5 65.9 all-reduce.3
  505.9 78.2 all-reduce.5
where the time goes:
time: 595 us; the launch traced here: 594 us
  waiting for transfers between devices  462 us (78%)
  matrix products  49.6 us (8%)
  other arithmetic  29.7 us (5%)
  blocking collectives  24.9 us (4%)
  between operations  14.5 us (2%)
  local copies, waits for them, and re-layouts  12.9 us (2%)
    reduce_scatter x1, waiting for transfers between devices, body(): lax.psum_scatter(apply_block(block_real, block_imag, needed), 'col', scat...  210 us
    all_gather x1, waiting for transfers between devices, body(): gathered = lax.all_gather(owned, ('row', 'col'), axis=0, tiled=True)  117 us
    psum x1, waiting for transfers between devices, body(): totals = lax.psum((column_density, pivot_density), 'pole')  75 us
    psum x1, waiting for transfers between devices, body(): pivot = inverse - lax.psum(pivot_term(owned, column), ('row', 'col'))  60.3 us
    dot_general x1, matrix products, apply_block(): second = jnp.dot(block_imag, flat, preferred_element_type=jnp.float32)  15.2 us
    dot_general x4, matrix products, precise(): jnp.dot(left, right, precision=lax.Precision.HIGHEST, preferred_element_t...  14.8 us
    all_gather x1, blocking collectives, body(): lax.all_gather(margin_panel, 'pole', axis=1, tiled=True)  13.8 us
    dot_general x1, matrix products, apply_block(): first = jnp.dot(block_real, flat, preferred_element_type=jnp.float32)  12.5 us
  transfers between devices with their start and end apart: 4, of which 4 were waited for; matrix products, arithmetic and copies ran while one was open for 1% of the time, Pallas kernels for 0%

commit v1 on v0

--- a/solution.py
+++ b/solution.py
@@ -68,7 +68,7 @@
     column = lax.psum_scatter(
         apply_block(block_real, block_imag, needed), "col", scatter_dimension=0, tiled=True
     )
-    pivot = inverse - lax.psum(pivot_term(owned, column), ("row", "col"))
+    pivot = inverse - lax.psum(lax.psum(pivot_term(owned, column), "col"), "row")
     column_density = weight[0] * column[:, 0] - weight[1] * column[:, 1]
     pivot_density = weight[0] * pivot[0] - weight[1] * pivot[1]
     totals = lax.psum((column_density, pivot_density), "pole")

time: 595 us -> 640 us (1.076)
  waiting for transfers between devices: 462 us -> 508 us
    psum x1 -> x2, waiting for transfers between devices: 60.3 us -> 105 us  [the longest x1 87.6 us: body(): lax.psum(pivot_term(owned, column), 'col')]
  transfers between devices with their start and end apart: 4 -> 5, of which waited for: 4 -> 5; matrix products, arithmetic and copies ran while one was open for 1% -> 1% of each run, Pallas kernels for 0% -> 0%
where the time goes in v1:
time: 640 us
  waiting for transfers between devices  508 us (79%)
  matrix products  49.6 us (8%)
  other arithmetic  29.6 us (5%)
  blocking collectives  24.9 us (4%)
  between operations  14.5 us (2%)
  local copies, waits for them, and re-layouts  12.3 us (2%)
    reduce_scatter x1, waiting for transfers between devices, body(): lax.psum_scatter(apply_block(block_real, block_imag, needed), 'col', scat...  210 us
    all_gather x1, waiting for transfers between devices, body(): gathered = lax.all_gather(owned, ('row', 'col'), axis=0, tiled=True)  117 us
    psum x1, waiting for transfers between devices, body(): lax.psum(pivot_term(owned, column), 'col')  87.6 us
    psum x1, waiting for transfers between devices, body(): totals = lax.psum((column_density, pivot_density), 'pole')  76.6 us
    psum x1, waiting for transfers between devices, body(): lax.psum(lax.psum(pivot_term(owned, column), 'col'), 'row')  17.1 us
    dot_general x1, matrix products, apply_block(): second = jnp.dot(block_imag, flat, preferred_element_type=jnp.float32)  15.2 us
    dot_general x4, matrix products, precise(): jnp.dot(left, right, precision=lax.Precision.HIGHEST, preferred_element_t...  14.8 us
    all_gather x1, blocking collectives, body(): lax.all_gather(margin_panel, 'pole', axis=1, tiled=True)  13.8 us
  transfers between devices with their start and end apart: 5, of which 5 were waited for; matrix products, arithmetic and copies ran while one was open for 1% of the time, Pallas kernels for 0%

profile of v1, /device:TPU:0, one launch (start us, length us, event | category | flops | bytes accessed | tf_op | source)
XLA Modules:
  0.0 639.9 jit_solution(4639005313834560345)
XLA Ops:
  7.2 13.8 %all_gather.10 = bf16[768,512]{1,0:T(8,128)(2,1)S(1)} all-gather(bf16[768,128]{1,0:T(8,128)(2,1)} %param.7), channel_id=1, replica_groups=mesh['pole'=4,'row'=2,'col'=4] {'pole'}, dimensions={1}, use_global_device_ids=true | all-gather | bytes 983040 | tf_op jit(solution)/shard_map/all_gather | solution.py:61
  21.0 1.3 fusion.42
  22.3 11.1 %all_gather.9 = bf16[768,512]{1,0:T(8,128)(2,1)S(1)} all-gather(bf16[768,128]{1,0:T(8,128)(2,1)} %param.6), channel_id=1, replica_groups=mesh['pole'=4,'row'=2,'col'=4] {'pole'}, dimensions={1}, use_global_device_ids=true | all-gather | bytes 983040 | tf_op jit(solution)/shard_map/all_gather | solution.py:60
  33.4 5.0 fusion.21
  38.4 3.7 fusion.19
  42.8 3.1 fusion.23
  45.8 3.1 fusion.24
  48.9 1.5 pad_maximum_fusion.1
  50.4 0.0 reduce-scatter.2.cloned.1.call-start
  50.4 117.1 %all-gather.2.cloned.1.call-done = bf16[6144,2,512]{0,2,1:T(8,128)(2,1)} async-done(((bf16[768,2,512]{0,2,1:T(8,128)(2,1)}), bf16[6144,2,512]{0,2,1:T(8,128)(2,1)}) %all-gather.2.cloned.1.call-update) | async-done | bytes 12582928 | tf_op jit(solution)/shard_map/all_gather | solution.py:64
  167.5 2.1 constant_dynamic-slice_fusion.2
  169.6 12.5 %fusion.6 = f32[3072,1024]{0,1:T(8,128)S(1)} fusion(bf16[1536,1024]{0,1:T(8,128)(2,1)S(1)} %bitcast.59, bf16[1,2,3072,1536]{3,2,1,0:T(8,128)(2,1)} %param.11), kind=kOutput, calls=%fused_computation.7 | convolution fusion | flops 9663676416 | bytes 25165824 | tf_op jit(solution)/shard_map/dot_general | solution.py:26
  182.1 15.2 %fusion.9 = f32[3072,1024]{0,1:T(8,128)} fusion(bf16[1536,1024]{0,1:T(8,128)(2,1)S(1)} %bitcast.60, bf16[1,2,3072,1536]{3,2,1,0:T(8,128)(2,1)} %param.11), kind=kOutput, calls=%fused_computation.8 | convolution fusion | flops 9663676416 | bytes 25165824 | tf_op jit(solution)/shard_map/dot_general | solution.py:27
  197.3 7.4 %fusion.13 = (f32[3072,1,512]{0,2,1:T(8,128)S(1)}, f32[3072,1,512]{0,2,1:T(8,128)}) fusion(f32[3072,1024]{0,1:T(8,128)} %fusion.9, f32[3072,1024]{0,1:T(8,128)S(1)} %fusion.6), kind=kLoop, calls=%fused_computation.12 | loop fusion | flops 3145728 | bytes 37748736 | tf_op jit(solution)/shard_map/stack | solution.py:28
  204.8 9.2 %maximum_negate_fusion = f32[3072,2,512]{0,2,1:T(8,128)} fusion(f32[3072,1,512]{0,2,1:T(8,128)} %get-tuple-element.11, f32[3072,1,512]{0,2,1:T(8,128)S(1)} %get-tuple-element.10), kind=kLoop, calls=%fused_computation | loop fusion | flops 6291456 | bytes 25165824 | tf_op jit(solution)/shard_map/neg | solution.py:28
  214.0 0.3 all-reduce.5.cloned.1.call-start
  214.2 209.9 %reduce-scatter.2.cloned.1.call-done = f32[768,2,512]{0,2,1:T(8,128)} async-done(((f32[3072,2,512]{0,2,1:T(8,128)}), f32[768,2,512]{0,2,1:T(8,128)}) %reduce-scatter.2.cloned.1.call-update) | async-done | bytes 3145744 | tf_op jit(solution)/shard_map/reduce_scatter | solution.py:68
  424.2 7.1 %fusion.43 = f32[1024,1024]{1,0:T(8,128)S(1)} fusion(bf16[768,1024]{0,1:T(8,128)(2,1)S(1)} %bitcast.58, f32[768,1024]{0,1:T(8,128)} %bitcast.55), kind=kOutput, calls=%fused_computation.56 | convolution fusion | flops 9663676416 | bytes 8912896 | tf_op jit(solution)/shard_map/dot_general | solution.py:37
  431.3 0.5 fusion.28
  431.8 1.5 pad_maximum_fusion
  433.4 87.6 %all-reduce.5.cloned.1.call-done = f32[2,512,512]{2,1,0:T(8,128)} async-done(((f32[2,512,512]{2,1,0:T(8,128)}), f32[2,512,512]{2,1,0:T(8,128)}) %all-reduce.5.cloned.1.call-update) | async-done | bytes 2097168 | tf_op jit(solution)/shard_map/psum | solution.py:71
  521.1 0.6 fusion.41
  521.7 4.7 fusion.18
  526.4 17.1 %all-reduce.7.cloned.1.call-done = f32[2,512,512]{2,1,0:T(8,128)} async-done(((f32[2,512,512]{2,1,0:T(8,128)}), f32[2,512,512]{2,1,0:T(8,128)}) %all-reduce.7.cloned.1.call-update) | async-done | bytes 2097168 | tf_op jit(solution)/shard_map/psum | solution.py:71
  543.6 2.1 bitcast_subtract_fusion
  545.7 1.3 copy-done.3
  547.0 2.8 fusion.26
  549.8 3.4 copy.10
  553.2 76.6 %all-reduce.9.cloned.1.call-done = (f32[768,512]{0,1:T(8,128)}, f32[512,512]{1,0:T(8,128)}) async-done(((f32[768,512]{0,1:T(8,128)}, f32[512,512]{1,0:T(8,128)}), (f32[768,512]{0,1:T(8,128)}, f32[512,512]{1,0:T(8,128)})) %all-reduce.9.cloned.1.call-update) | async-done | bytes 2621456 | tf_op jit(solution)/shard_map/psum | solution.py:74
  629.7 1.0 constant_dynamic-slice_fusion.1
  630.8 0.9 copy.11
  631.7 1.7 constant_dynamic-slice_fusion
  (19 shorter events, 0.2 us)
Async XLA Ops:
  7.2 160.4 %all-gather.2.cloned.1.call-start = ((), (), s32[]{:S(2)}) async-start(), calls=%async_computation.1 | async-start | bytes 14155776 | tf_op jit(solution)/shard_map/all_gather | solution.py:64
  33.4 5.0 copy-start
  50.4 373.8 %reduce-scatter.2.cloned.1.call-start = ((), (), s32[]{:S(2)}) async-start(), calls=%async_computation.2 | async-start | bytes 15728640 | tf_op jit(solution)/shard_map/reduce_scatter | solution.py:68
  213.9 210.2 %copy-start.4 = (bf16[768,2,512]{0,2,1:T(8,128)(2,1)S(1)}, bf16[768,2,512]{0,2,1:T(8,128)(2,1)}, u32[]{:S(2)}) copy-start(bf16[768,2,512]{0,2,1:T(8,128)(2,1)} %pad_maximum_fusion.1) | copy-start | bytes 4718596
  214.0 307.1 %all-reduce.5.cloned.1.call-start = ((), (), s32[]{:S(2)}) async-start(), calls=%async_computation.3 | async-start | bytes 4194304 | tf_op jit(solution)/shard_map/psum | solution.py:71
  433.3 87.8 %copy-start.5 = (f32[1,2]{1,0:T(1,128)S(1)}, f32[1,2]{1,0:T(1,128)}, u32[]{:S(2)}) copy-start(f32[1,2]{1,0:T(1,128)} %param.9) | copy-start | bytes 28
  433.4 110.2 %all-reduce.7.cloned.1.call-start = ((), (), s32[]{:S(2)}) async-start(), calls=%async_computation.4 | async-start | bytes 4194304 | tf_op jit(solution)/shard_map/psum | solution.py:71
  521.1 108.7 %all-reduce.9.cloned.1.call-start = ((), (), s32[]{:S(2)}) async-start(), calls=%async_computation.5 | async-start | bytes 5242880 | tf_op jit(solution)/shard_map/psum | solution.py:74
  521.7 21.9 %copy-start.1 = (f32[1,2,512,512]{3,2,1,0:T(8,128)S(1)}, f32[1,2,512,512]{3,2,1,0:T(8,128)}, u32[]{:S(2)}) copy-start(f32[1,2,512,512]{3,2,1,0:T(8,128)} %param.10) | copy-start | bytes 6291460
  545.7 1.3 copy-start.3
  547.0 2.8 copy-start.2
Sparse Core Ops, SparseCore 0:
  50.5 116.9 all-gather.1
  214.1 210.0 reduce-scatter.1
  433.5 87.5 all-reduce.4
  523.4 20.1 all-reduce.6
  549.9 79.7 all-reduce.8
